TPU v7x, 256 devices: a whole 4x4x8 slice. The times are simulated.
256 devices in a mesh: dp: 8 (over z_hi, x), expert: 32 (over y, z_lo, core).
Axes of the slice: x: 4, y: 4, z: 8 (z_hi: 2, z_lo: 4; z = z_hi * 4 + z_lo), core: 2. Of those that a mesh axis runs over, the one named last changes fastest.
Arguments:
- tokens_x: bfloat16 [4096, 4096], P('expert'), may hold values from -6 to 6
- cotangent: bfloat16 [4096, 4096], P('expert'), may hold values from -1.5 to 1.5
- expert_ids: int32 [4096, 2], P('expert'), may hold values from 0 to 31, all different within a row; in each aligned block of 128 rows (0 to 127, 128 to 255, ...) at most 16 rows name the same one
- gate_weights: float32 [4096, 2], P('expert'), may hold values from 0.1 to 1
- w_gate: bfloat16 [32, 1536, 4096], P('expert', 'dp'), may hold values from -0.09375 to 0.09375
- w_up: bfloat16 [32, 1536, 4096], P('expert', 'dp'), may hold values from -0.09375 to 0.09375
- w_down: bfloat16 [32, 1536, 4096], P('expert', 'dp'), may hold values from -0.15625 to 0.15625
Outputs:
- grad_tokens: bfloat16 [4096, 4096], P('expert', 'dp')
- grad_gate: bfloat16 [32, 1536, 4096], P('expert', 'dp')
- grad_up: bfloat16 [32, 1536, 4096], P('expert', 'dp')
- grad_down: bfloat16 [32, 1536, 4096], P('expert', 'dp')
Inputs may be any that keep to these rules, and one draw needn't show every extreme that they name: `expert_ids`: within the rows of one device (aligned blocks of 128 tokens) no expert is named by more than 16 routes, a bound that some block reaches; the routes of a token name different experts.
All inputs are finite; a program needn't handle non-finite values.
Results may differ from a plain program's by a relative error of at most 0.017.
Values may be sent and summed in bfloat16 or wider, within the bound.
A program may use at most 128 MiB of HBM per device.

v0:
```python
import jax
import jax.numpy as jnp
from jax import lax
from jax.sharding import PartitionSpec as P


def contract(left, right, left_dim, right_dim):
    return lax.dot_general(
        left, right, (((left_dim,), (right_dim,)), ((), ())), preferred_element_type=jnp.float32
    )


def expert_block(inputs, scaled, weight_gate, weight_up, weight_down):
    gate_pre = contract(inputs, weight_gate, 1, 1)
    up_pre = contract(inputs, weight_up, 1, 1)
    sigmoid = jax.nn.sigmoid(gate_pre)
    swish_value = gate_pre * sigmoid
    activation = (swish_value * up_pre).astype(jnp.bfloat16)
    act_grad = contract(scaled, weight_down, 1, 1)
    slope_term = sigmoid * (1.0 + gate_pre * (1.0 - sigmoid))
    gate_grad = (act_grad * up_pre * slope_term).astype(jnp.bfloat16)
    up_grad = (act_grad * swish_value).astype(jnp.bfloat16)
    grad_gate = contract(gate_grad, inputs, 0, 0)
    grad_up = contract(up_grad, inputs, 0, 0)
    grad_down = contract(activation, scaled, 0, 0)
    partial_rows = contract(gate_grad, weight_gate, 1, 0) + contract(up_grad, weight_up, 1, 0)
    return ((grad_gate, grad_up, grad_down), partial_rows)


def local(tokens_x, cotangent, expert_ids, gate_weights, w_gate, w_up, w_down):
    axis_width = lax.axis_size("expert")
    row_count, route_count = expert_ids.shape
    model_width = tokens_x.shape[1]
    capacity = 2 * row_count * route_count // axis_width
    flat_ids = expert_ids.reshape(-1)
    one_hot = (flat_ids[:, None] == jnp.arange(axis_width, dtype=jnp.int32)[None, :]).astype(
        jnp.int32
    )
    earlier = jnp.cumsum(one_hot, axis=0) - one_hot
    rank_index = jnp.sum(earlier * one_hot, axis=1)
    slot_index = flat_ids * capacity + rank_index
    slot_route = (
        jnp.full((axis_width * capacity,), -1, jnp.int32)
        .at[slot_index]
        .set(jnp.arange(row_count * route_count, dtype=jnp.int32))
    )
    filled = slot_route >= 0
    safe_route = jnp.maximum(slot_route, 0)
    token_of = safe_route // route_count
    sent_inputs = jnp.where(filled[:, None], tokens_x[token_of], jnp.zeros((), jnp.bfloat16))
    route_gate = gate_weights.reshape(-1)[safe_route]
    sent_scaled = jnp.where(
        filled[:, None], route_gate[:, None] * cotangent[token_of].astype(jnp.float32), 0.0
    ).astype(jnp.bfloat16)
    arrived_inputs, arrived_scaled = (
        lax.all_to_all(
            sent_inputs.reshape(axis_width, capacity, model_width),
            "expert",
            split_axis=0,
            concat_axis=0,
            tiled=True,
        ),
        lax.all_to_all(
            sent_scaled.reshape(axis_width, capacity, model_width),
            "expert",
            split_axis=0,
            concat_axis=0,
            tiled=True,
        ),
    )
    arrived_inputs = arrived_inputs.reshape(axis_width * capacity, model_width)
    arrived_scaled = arrived_scaled.reshape(axis_width * capacity, model_width)
    own_gate = w_gate[0]
    own_up = w_up[0]
    own_down = w_down[0]
    all_grads, partial_rows = expert_block(
        arrived_inputs, arrived_scaled, own_gate, own_up, own_down
    )
    grad_gate, grad_up, grad_down = all_grads
    returned = lax.all_to_all(
        partial_rows.astype(jnp.bfloat16).reshape(axis_width, capacity, model_width),
        "expert",
        split_axis=0,
        concat_axis=0,
        tiled=True,
    )
    picked = returned.reshape(axis_width * capacity, model_width)[slot_index].astype(jnp.float32)
    combined = jnp.sum(picked.reshape(row_count, route_count, model_width), axis=1)
    grad_tokens = lax.psum_scatter(
        combined.astype(jnp.bfloat16), "dp", scatter_dimension=1, tiled=True
    )
    return (
        grad_tokens,
        grad_gate[None].astype(jnp.bfloat16),
        grad_up[None].astype(jnp.bfloat16),
        grad_down[None].astype(jnp.bfloat16),
    )


def solution(mesh):
    placed = (
        P("expert", None),
        P("expert", None),
        P("expert", None),
        P("expert", None),
        P("expert", "dp", None),
        P("expert", "dp", None),
        P("expert", "dp", None),
    )
    return jax.shard_map(
        local,
        mesh=mesh,
        in_specs=placed,
        out_specs=(
            P("expert", "dp"),
            P("expert", "dp", None),
            P("expert", "dp", None),
            P("expert", "dp", None),
        ),
        check_vma=False,
    )
```

profile of v0, /device:TPU:2, one launch (start us, length us, event | category | flops | bytes accessed | tf_op | source)
XLA Modules:
  0.0 452.3 jit_solution(10250103584700221324)
XLA Ops:
  7.2 0.8 broadcast_multiply_fusion
  8.0 0.8 copy.12
  8.8 0.1 eq.29
  8.9 0.1 eq.25
  9.2 0.1 mul.53
  9.3 0.6 reduce-window.6
  9.9 0.2 slice_reduce_fusion
  10.3 1.4 scatter_custom_fusion
  11.8 9.9 %gather_fusion.2 = bf16[512,4096]{1,0:T(8,128)(2,1)} fusion(bf16[128,4096]{1,0:T(8,128)(2,1)} %param.7, s32[1024]{0:T(1024)S(1)} %get-tuple-element.8), kind=kCustom, calls=%fused_computation.2 | custom fusion | bytes 8390656 | tf_op jit(solution)/shard_map/gather | solution.py:50
  21.7 4.5 broadcast_select_fusion
  26.2 9.2 %all-to-all-start.1 = ((bf16[32,16,4096]{2,1,0:T(8,128)(2,1)}), bf16[32,16,4096]{2,1,0:T(8,128)(2,1)}, u32[]{:S(2)}, u32[]{:S(2)}) async-start(bf16[32,16,4096]{2,1,0:T(8,128)(2,1)} %broadcast_select_fusion), calls=%async_computation.1 | async-start | bytes 8388608 | tf_op jit(solution)/shard_map/all_to_all | solution.py:56
  35.5 0.1 reshape.97
  35.7 3.5 gather_fusion
  39.3 4.4 gather_fusion.1
  43.7 6.3 %fusion.1 = bf16[32,16,4096]{2,1,0:T(8,128)(2,1)} fusion(bf16[32,16,4096]{2,1,0:T(8,128)(2,1)} %bitcast.61, f32[32,16]{1,0:T(8,128)S(1)} %mul.55, pred[32,16]{1,0:T(8,128)(4,1)S(1)} %broadcast_in_dim.44), kind=kLoop, calls=%fused_computation.7 | loop fusion | flops 8388608 | bytes 8391168 | tf_op jit(solution)/shard_map/convert_element_type | solution.py:54
  50.0 80.8 %all-to-all-done.1 = bf16[32,16,4096]{2,1,0:T(8,128)(2,1)} async-done(((bf16[32,16,4096]{2,1,0:T(8,128)(2,1)}), bf16[32,16,4096]{2,1,0:T(8,128)(2,1)}, u32[]{:S(2)}, u32[]{:S(2)}) %all-to-all-start.1) | async-done | bytes 4194336 | tf_op jit(solution)/shard_map/all_to_all | solution.py:56
  130.8 5.0 %all-to-all-start = ((bf16[32,16,4096]{2,1,0:T(8,128)(2,1)}), bf16[32,16,4096]{2,1,0:T(8,128)(2,1)}, u32[]{:S(2)}, u32[]{:S(2)}) async-start(bf16[32,16,4096]{2,1,0:T(8,128)(2,1)} %fusion.1), calls=%async_computation | async-start | bytes 8388608 | tf_op jit(solution)/shard_map/all_to_all | solution.py:63
  135.9 4.6 %fusion.7 = f32[512,192]{0,1:T(8,128)} fusion(bf16[512,4096]{1,0:T(8,128)(2,1)} %bitcast.7, bf16[1,192,4096]{2,1,0:T(8,128)(2,1)S(1)} %copy-done), kind=kOutput, calls=%fused_computation.18 | convolution fusion | flops 805306368 | bytes 6160384 | tf_op jit(solution)/shard_map/dot_general | solution.py:8
  140.5 4.5 fusion.10
  144.9 86.1 %all-to-all-done = bf16[32,16,4096]{2,1,0:T(8,128)(2,1)} async-done(((bf16[32,16,4096]{2,1,0:T(8,128)(2,1)}), bf16[32,16,4096]{2,1,0:T(8,128)(2,1)}, u32[]{:S(2)}, u32[]{:S(2)}) %all-to-all-start) | async-done | bytes 4194336 | tf_op jit(solution)/shard_map/all_to_all | solution.py:63
  231.1 4.4 multiply_convert_fusion.1
  235.5 1.3 fusion.5
  236.8 3.3 add_convert_fusion
  240.1 4.9 %all-to-all-start.2 = ((bf16[32,16,4096]{2,1,0:T(8,128)(2,1)}), bf16[32,16,4096]{2,1,0:T(8,128)(2,1)}, u32[]{:S(2)}, u32[]{:S(2)}) async-start(bf16[32,16,4096]{2,1,0:T(8,128)(2,1)} %bitcast.60), calls=%async_computation.2 | async-start | bytes 8388608 | tf_op jit(solution)/shard_map/all_to_all | solution.py:80
  245.0 95.3 %all-to-all-done.2 = bf16[32,16,4096]{2,1,0:T(8,128)(2,1)} async-done(((bf16[32,16,4096]{2,1,0:T(8,128)(2,1)}), bf16[32,16,4096]{2,1,0:T(8,128)(2,1)}, u32[]{:S(2)}, u32[]{:S(2)}) %all-to-all-start.2) | async-done | bytes 4194336 | tf_op jit(solution)/shard_map/all_to_all | solution.py:80
  340.3 8.0 %gather_fusion.3 = bf16[256,4096]{1,0:T(8,128)(2,1)} fusion(bf16[512,4096]{1,0:T(8,128)(2,1)} %bitcast.11, s32[1024]{0:T(1024)S(1)} %pad_clamp_fusion), kind=kCustom, calls=%fused_computation.3 | custom fusion | bytes 4195328 | tf_op jit(solution)/shard_map/gather | solution.py:87
  348.3 4.4 gather.21
  352.7 7.7 %reduce_sum.25 = bf16[128,4096]{1,0:T(8,128)(2,1)} reduce(bf16[128,2,4096]{2,1,0:T(2,128)(2,1)} %gather.21, bf16[]{:T(256)} %constant.37.clone.1), dimensions={1}, to_apply=%region_4.5 | reduce | flops 524288 | bytes 3145730 | tf_op jit(solution)/shard_map/reduce_sum | solution.py:88
  360.4 4.3 fusion.3
  364.8 4.4 fusion.2
  369.2 4.4 fusion.4
  373.6 71.9 %reduce-scatter.2.cloned.1.call-done = bf16[128,512]{1,0:T(8,128)(2,1)} async-done(((bf16[128,4096]{1,0:T(8,128)(2,1)}), bf16[128,512]{1,0:T(8,128)(2,1)}) %reduce-scatter.2.cloned.1.call-update) | async-done | bytes 131088 | tf_op jit(solution)/shard_map/reduce_scatter | solution.py:89
  (28 shorter events, 0.7 us)
Async XLA Ops:
  7.2 128.7 %copy-start = (bf16[1,192,4096]{2,1,0:T(8,128)(2,1)S(1)}, bf16[1,192,4096]{2,1,0:T(8,128)(2,1)}, u32[]{:S(2)}) copy-start(bf16[1,192,4096]{2,1,0:T(8,128)(2,1)} %param.11) | copy-start | bytes 4718596
  26.2 9.2 %copy-start.5 = (f32[128,2]{0,1:T(2,128)S(1)}, f32[128,2]{0,1:T(2,128)}, u32[]{:S(2)}) copy-start(f32[128,2]{0,1:T(2,128)} %param.10) | copy-start | bytes 3076
  26.2 13.1 %copy-start.1 = (bf16[128,4096]{1,0:T(8,128)(2,1)S(1)}, bf16[128,4096]{1,0:T(8,128)(2,1)}, u32[]{:S(2)}) copy-start(bf16[128,4096]{1,0:T(8,128)(2,1)} %param.8) | copy-start | bytes 3145732
  26.2 104.6 %all-to-all-start.1 = ((bf16[32,16,4096]{2,1,0:T(8,128)(2,1)}), bf16[32,16,4096]{2,1,0:T(8,128)(2,1)}, u32[]{:S(2)}, u32[]{:S(2)}) async-start(bf16[32,16,4096]{2,1,0:T(8,128)(2,1)} %broadcast_select_fusion), calls=%async_computation.1 | async-start | bytes 8388608 | tf_op jit(solution)/shard_map/all_to_all | solution.py:56
  130.8 100.2 %all-to-all-start = ((bf16[32,16,4096]{2,1,0:T(8,128)(2,1)}), bf16[32,16,4096]{2,1,0:T(8,128)(2,1)}, u32[]{:S(2)}, u32[]{:S(2)}) async-start(bf16[32,16,4096]{2,1,0:T(8,128)(2,1)} %fusion.1), calls=%async_computation | async-start | bytes 8388608 | tf_op jit(solution)/shard_map/all_to_all | solution.py:63
  135.8 4.6 %copy-start.2 = (bf16[1,192,4096]{2,1,0:T(8,128)(2,1)S(1)}, bf16[1,192,4096]{2,1,0:T(8,128)(2,1)}, u32[]{:S(2)}) copy-start(bf16[1,192,4096]{2,1,0:T(8,128)(2,1)} %param.12) | copy-start | bytes 4718596
  240.1 100.3 %all-to-all-start.2 = ((bf16[32,16,4096]{2,1,0:T(8,128)(2,1)}), bf16[32,16,4096]{2,1,0:T(8,128)(2,1)}, u32[]{:S(2)}, u32[]{:S(2)}) async-start(bf16[32,16,4096]{2,1,0:T(8,128)(2,1)} %bitcast.60), calls=%async_computation.2 | async-start | bytes 8388608 | tf_op jit(solution)/shard_map/all_to_all | solution.py:80
  244.9 200.5 %reduce-scatter.2.cloned.1.call-start = ((), (), s32[]{:S(2)}) async-start(), calls=%async_computation.4 | async-start | bytes 1179648 | tf_op jit(solution)/shard_map/reduce_scatter | solution.py:89
  364.8 4.4 copy-start.3
  364.8 4.4 copy-start.4
Sparse Core Ops, SparseCore 0:
  360.6 84.8 reduce-scatter.1
where the time goes:
time: 453 us; the launch traced here: 452 us
  waiting for transfers between devices  334 us (74%)
  local copies, waits for them, and re-layouts  33.6 us (7%)
  matrix products  31.2 us (7%)
  other arithmetic  20.1 us (4%)
  starting transfers between devices  19.1 us (4%)
  between operations  14.2 us (3%)
    all_to_all x1, waiting for transfers between devices, local(): lax.all_to_all(partial_rows.astype(jnp.bfloat16).reshape(axis_width, capa...  95.3 us
    all_to_all x1, waiting for transfers between devices, local(): lax.all_to_all(sent_scaled.reshape(axis_width, capacity, model_width), 'e...  86.1 us
    all_to_all x1, waiting for transfers between devices, local(): lax.all_to_all(sent_inputs.reshape(axis_width, capacity, model_width), 'e...  80.8 us
    reduce_scatter x1, waiting for transfers between devices, local(): lax.psum_scatter(combined.astype(jnp.bfloat16), 'dp', scatter_dimension=1...  71.9 us
    dot_general x8, matrix products, contract(): lax.dot_general(left, right, (((left_dim,), (right_dim,)), ((), ())), pre...  31.2 us
    gather x2, local copies, waits for them, and re-layouts, local(): returned.reshape(axis_width * capacity, model_width)[slot_index]  12.4 us
    gather x1, local copies, waits for them, and re-layouts, local(): tokens_x[token_of]  9.92 us
    all_to_all x1, starting transfers between devices, local(): lax.all_to_all(sent_inputs.reshape(axis_width, capacity, model_width), 'e...  9.18 us
  transfers between devices with their start and end apart: 4, of which 4 were waited for; matrix products, arithmetic and copies ran while one was open for 8% of the time, Pallas kernels for 0%

commit v1 on v0

v1 whole, which is shorter than its diff:
```python
import functools

import jax
import jax.numpy as jnp
from jax import lax
from jax.experimental import pallas as pl
from jax.experimental.pallas import tpu as pltpu
from jax.sharding import PartitionSpec as P

MESH = pl.DeviceIdType.MESH
F32, BF16 = jnp.float32, jnp.bfloat16
D = 4096
HALF = 2048
QUARTER = 1024
BLOCK = 512
FF = 192
TOK = 128
CAP = 16
EXPERTS = 32
ROWS = EXPERTS * CAP
CHUNKS = 4
PER = EXPERTS // CHUNKS
CROWS = ROWS // CHUNKS

Z_C = ((1, 0), (-1, 0), (2, 0), (0, 1), (-1, 1), (1, 1), (-2, 1), (0, 0))
MESSAGES = tuple(
    (dy,) + Z_C[(k + 2 * n) % 8] for k in range(8) for n, dy in enumerate((1, 3, 2, 0))
)
SELF = MESSAGES.index((0, 0, 0))
REMOTE = tuple(i for i in range(EXPERTS) if i != SELF)


def nt(left, right):
    return lax.dot_general(left, right, (((1,), (1,)), ((), ())), preferred_element_type=F32)


def nn(left, right):
    return lax.dot_general(left, right, (((1,), (0,)), ((), ())), preferred_element_type=F32)


def tn(left, right):
    return lax.dot_general(left, right, (((0,), (0,)), ((), ())), preferred_element_type=F32)


def kernel(
    route_ref, tok_hbm, cot_hbm, wg_hbm, wu_hbm, wd_hbm,
    gt_ref, gg_hbm, gu_hbm, gd_hbm,
    tok, weights, onehot, gates, sent, arrived, act, ggrad, ugrad,
    part_own, part_out, part_in, summed, returned, combined, fin_out, fin_in, grads,
    tok_sem, w_sem, self_sem, a_send, a_recv, x_send, x_recv, p_send, p_recv, r_send, r_recv, f_send, f_recv, g_sem,
):
    dp, ex = lax.axis_index("dp"), lax.axis_index("expert")
    h, x = dp // 4, dp % 4
    y, l, c = ex // 8, (ex // 2) % 4, ex % 2
    z = h * 4 + l
    p = x % 2
    q = 1 - p

    def at(dx, dy, dz, dc):
        zz = (z + dz + 8) % 8
        return (
            (zz // 4) * 4 + (x + dx + 4) % 4,
            ((y + dy + 4) % 4) * 8 + (zz % 4) * 2 + (c + dc) % 2,
        )

    ins = []
    for i, src in enumerate((tok_hbm, cot_hbm)):
        for j in range(4):
            cols = pl.ds(pl.multiple_of((2 * j + p) * BLOCK, BLOCK), BLOCK)
            ins.append(
                pltpu.make_async_copy(
                    src.at[:, cols], tok.at[i, :, pl.ds(j * BLOCK, BLOCK)], tok_sem.at[4 * i + j]
                )
            )
    w_ins = []
    for i, src in enumerate((wg_hbm, wu_hbm, wd_hbm)):
        for b in range(8):
            w_ins.append(
                pltpu.make_async_copy(
                    src.at[:, pl.ds(b * BLOCK, BLOCK)],
                    weights.at[i, b % 2, :, pl.ds((b // 2) * BLOCK, BLOCK)],
                    w_sem.at[8 * i + b],
                )
            )
    for copy in ins:
        copy.start()
    for copy in w_ins:
        copy.start()

    barrier = pltpu.get_barrier_semaphore()
    peers = [(0,) + MESSAGES[i] for i in REMOTE]
    peers += [(0, dy, -dz, dc) for dy, dz, dc in MESSAGES if abs(dz) == 2]
    peers += [(1, 0, 0, 0), (-1, 0, 0, 0), (2, 0, 0, 0), (0, 0, 4, 0), (2, 0, 4, 0)]
    for peer in peers:
        pl.semaphore_signal(barrier, inc=1, device_id=at(*peer), device_id_type=MESH)

    ids0, ids1 = route_ref[0:1, :], route_ref[1:2, :]
    gate0, gate1 = route_ref[2:3, :], route_ref[3:4, :]
    expert_row = lax.broadcasted_iota(jnp.int32, (EXPERTS, TOK), 0).astype(F32)
    earlier = (
        lax.broadcasted_iota(jnp.int32, (TOK, TOK), 0)
        < lax.broadcasted_iota(jnp.int32, (TOK, TOK), 1)
    )
    earlier = jnp.where(earlier, 1.0, 0.0).astype(BF16)
    hot0 = jnp.where(expert_row == ids0, 1.0, 0.0)
    hot1 = jnp.where(expert_row == ids1, 1.0, 0.0)
    before0 = nn(hot0.astype(BF16), earlier)
    before1 = nn(hot1.astype(BF16), earlier) + jnp.sum(hot0, axis=1, keepdims=True)
    rank0 = jnp.sum(hot0 * before0, axis=0, keepdims=True)
    rank1 = jnp.sum(hot1 * before1, axis=0, keepdims=True)
    slot_row = lax.broadcasted_iota(jnp.int32, (CAP, TOK), 0).astype(F32)
    for i, (dy, dz, dc) in enumerate(MESSAGES):
        expert = (((y + dy) % 4) * 8 + ((l + dz + 4) % 4) * 2 + (c + dc) % 2).astype(F32)
        is0 = (slot_row == rank0) & (ids0 == expert)
        is1 = (slot_row == rank1) & (ids1 == expert)
        rows = pl.ds(i * CAP, CAP)
        onehot[rows, :] = jnp.where(is0 | is1, 1.0, 0.0)
        gate = jnp.where(is0, gate0, 0.0) + jnp.where(is1, gate1, 0.0)
        gates[rows, :] = jnp.broadcast_to(jnp.sum(gate, axis=1, keepdims=True), (CAP, TOK))

    def fwd(i):
        rows = pl.ds(i * CAP, CAP)
        return pltpu.make_async_remote_copy(
            sent.at[:, rows, :], arrived.at[p, :, rows, :], a_send.at[i], a_recv.at[i],
            device_id=at(0, *MESSAGES[i]), device_id_type=MESH,
        )

    own_rows = pl.ds(SELF * CAP, CAP)
    own_copy = pltpu.make_async_copy(
        sent.at[:, own_rows, :], arrived.at[p, :, own_rows, :], self_sem
    )

    for copy in ins:
        copy.wait()
    for ch in range(CHUNKS):
        rows = pl.ds(ch * CROWS, CROWS)
        pick = onehot[rows, :].astype(BF16)
        sent[0, rows, :] = nn(pick, tok[0]).astype(BF16)
        gate = gates[rows, 0:1]
        sent[1, rows, :] = (nn(pick, tok[1]) * gate).astype(BF16)
        if ch == 0:
            pl.semaphore_wait(barrier, len(peers))
        for i in range(ch * PER, (ch + 1) * PER):
            if i == SELF:
                own_copy.start()
            else:
                fwd(i).start()

    def sides(src, dst, ch, send, recv):
        rows = pl.ds(ch * CROWS, CROWS)
        copies = []
        for side, dx in enumerate((1, -1)):
            cols = pl.ds(side * QUARTER, QUARTER)
            copies.append(
                pltpu.make_async_remote_copy(
                    src(rows, cols), dst(rows, cols), send.at[2 * ch + side], recv.at[2 * ch + side],
                    device_id=at(dx, 0, 0, 0), device_id_type=MESH,
                )
            )
        return copies

    def spread(ch):
        ref = lambda rows, cols: arrived.at[p, :, rows, cols]
        return sides(ref, ref, ch, x_send, x_recv)

    def gather_recv(ch):
        ref = lambda rows, cols: arrived.at[q, :, rows, cols]
        return sides(ref, ref, ch, x_send, x_recv)

    def parts(ch):
        return sides(
            lambda rows, cols: part_out.at[rows, cols],
            lambda rows, cols: part_in.at[rows, cols], ch, p_send, p_recv,
        )

    def back(i):
        dy, dz, dc = MESSAGES[i]
        rows = pl.ds(i * CAP, CAP)
        return pltpu.make_async_remote_copy(
            summed.at[rows, :], returned.at[rows, :], r_send.at[i], r_recv.at[i],
            device_id=at(0, -dy, -dz, dc), device_id_type=MESH,
        )

    def take_in(ch):
        for i in range(ch * PER, (ch + 1) * PER):
            if i == SELF:
                own_copy.wait()
            else:
                fwd(i).wait_recv()
        for copy in spread(ch):
            copy.start()

    def compute(ch):
        for copy in gather_recv(ch):
            copy.wait_recv()
        rows = pl.ds(ch * CROWS, CROWS)
        gate_pre = nt(arrived[0, 0, rows, :], weights[0, 0]) + nt(arrived[1, 0, rows, :], weights[0, 1])
        up_pre = nt(arrived[0, 0, rows, :], weights[1, 0]) + nt(arrived[1, 0, rows, :], weights[1, 1])
        act_grad = nt(arrived[0, 1, rows, :], weights[2, 0]) + nt(arrived[1, 1, rows, :], weights[2, 1])
        s = jax.nn.sigmoid(gate_pre)
        swish = gate_pre * s
        act[rows, :] = (swish * up_pre).astype(BF16)
        gate_grad = (act_grad * up_pre * (s * (1.0 + gate_pre * (1.0 - s)))).astype(BF16)
        up_grad = (act_grad * swish).astype(BF16)
        ggrad[rows, :] = gate_grad
        ugrad[rows, :] = up_grad
        part_out[rows, :] = (nn(gate_grad, weights[0, q]) + nn(up_grad, weights[1, q])).astype(BF16)
        for copy in parts(ch):
            copy.start()
        part_own[rows, :] = nn(gate_grad, weights[0, p]) + nn(up_grad, weights[1, p])

    self_back = pltpu.make_async_copy(summed.at[own_rows, :], returned.at[own_rows, :], self_sem)

    def give_back(ch):
        for copy in parts(ch):
            copy.wait_recv()
        rows = pl.ds(ch * CROWS, CROWS)
        summed[rows, :] = (part_own[rows, :] + part_in[rows, :].astype(F32)).astype(BF16)
        for i in range(ch * PER, (ch + 1) * PER):
            if i == SELF:
                self_back.start()
            else:
                back(i).start()

    take_in(0)
    for copy in w_ins:
        copy.wait()
    for ch in range(1, CHUNKS + 2):
        if ch < CHUNKS:
            take_in(ch)
        if ch - 1 < CHUNKS:
            compute(ch - 1)
        if ch >= 2:
            give_back(ch - 2)

    outs = (gg_hbm, gu_hbm, gd_hbm)

    def grad_copy(i, b):
        return pltpu.make_async_copy(
            grads.at[i, b], outs[i].at[:, pl.ds(pl.multiple_of(b * BLOCK, BLOCK), BLOCK)], g_sem.at[i, b]
        )

    @pl.loop(0, 8)
    def _(b):
        half, cols = b % 2, pl.ds(pl.multiple_of((b // 2) * BLOCK, BLOCK), BLOCK)
        inputs = arrived[half, 0, :, cols]
        grads[0, b] = tn(ggrad[...], inputs).astype(BF16)
        grad_copy(0, b).start()
        grads[1, b] = tn(ugrad[...], inputs).astype(BF16)
        grad_copy(1, b).start()
        grads[2, b] = tn(act[...], arrived[half, 1, :, cols]).astype(BF16)
        grad_copy(2, b).start()

    self_back.wait()
    for i in REMOTE:
        back(i).wait_recv()
    fin_peers = ((2, 0, 0, 0), (0, 0, 4, 0), (2, 0, 4, 0))
    j_own = 2 * h + x // 2

    def fin(d):
        j_x, j_z = (x // 2 + d % 2) % 2, (h + d // 2) % 2
        return pltpu.make_async_remote_copy(
            fin_out.at[2 * j_z + j_x], fin_in.at[d - 1], f_send.at[d - 1], f_recv.at[d - 1],
            device_id=at(*fin_peers[d - 1]), device_id_type=MESH,
        )

    pick = onehot[...].T.astype(BF16)
    for j in range(4):
        block = nn(pick, returned[:, pl.ds(j * BLOCK, BLOCK)])
        combined[j] = block
        fin_out[j] = block.astype(BF16)
    for d in (3, 2, 1):
        fin(d).start()
    total = combined[j_own]
    for d in (1, 2, 3):
        fin(d).wait_recv()
        total += fin_in[d - 1].astype(F32)
    gt_ref[...] = total.astype(BF16)

    for i in REMOTE:
        fwd(i).wait_send()
        back(i).wait_send()
    for ch in range(CHUNKS):
        for copy in spread(ch) + parts(ch):
            copy.wait_send()
    for d in (1, 2, 3):
        fin(d).wait_send()

    @pl.loop(0, 8)
    def _(b):
        for i in range(3):
            grad_copy(i, b).wait()


def local(tokens_x, cotangent, expert_ids, gate_weights, w_gate, w_up, w_down):
    routes = jnp.concatenate([expert_ids.astype(F32), gate_weights], axis=1).T
    vmem = pl.BlockSpec(memory_space=pltpu.VMEM)
    anywhere = pl.BlockSpec(memory_space=pl.ANY)
    dma = pltpu.SemaphoreType.DMA
    grad = jax.ShapeDtypeStruct((FF, D), BF16)
    grad_tokens, grad_gate, grad_up, grad_down = pl.pallas_call(
        kernel,
        out_shape=(jax.ShapeDtypeStruct((TOK, BLOCK), BF16), grad, grad, grad),
        in_specs=[vmem] + [anywhere] * 5,
        out_specs=(vmem, anywhere, anywhere, anywhere),
        scratch_shapes=[
            pltpu.VMEM((2, TOK, HALF), BF16),
            pltpu.VMEM((3, 2, FF, HALF), BF16),
            pltpu.VMEM((ROWS, TOK), F32),
            pltpu.VMEM((ROWS, TOK), F32),
            pltpu.VMEM((2, ROWS, HALF), BF16),
            pltpu.VMEM((2, 2, ROWS, HALF), BF16),
            pltpu.VMEM((ROWS, FF), BF16),
            pltpu.VMEM((ROWS, FF), BF16),
            pltpu.VMEM((ROWS, FF), BF16),
            pltpu.VMEM((ROWS, HALF), F32),
            pltpu.VMEM((ROWS, HALF), BF16),
            pltpu.VMEM((ROWS, HALF), BF16),
            pltpu.VMEM((ROWS, HALF), BF16),
            pltpu.VMEM((ROWS, HALF), BF16),
            pltpu.VMEM((4, TOK, BLOCK), F32),
            pltpu.VMEM((4, TOK, BLOCK), BF16),
            pltpu.VMEM((3, TOK, BLOCK), BF16),
            pltpu.VMEM((3, 8, FF, BLOCK), BF16),
            dma((8,)), dma((24,)), dma,
            dma((EXPERTS,)), dma((EXPERTS,)),
            dma((2 * CHUNKS,)), dma((2 * CHUNKS,)),
            dma((2 * CHUNKS,)), dma((2 * CHUNKS,)),
            dma((EXPERTS,)), dma((EXPERTS,)),
            dma((3,)), dma((3,)), dma((3, 8)),
        ],
        name="expert_backward",
        compiler_params=pltpu.CompilerParams(
            collective_id=0, has_side_effects=True, vmem_limit_bytes=56 * 2**20
        ),
    )(routes, tokens_x, cotangent, w_gate[0], w_up[0], w_down[0])
    return grad_tokens, grad_gate[None], grad_up[None], grad_down[None]


def solution(mesh):
    placed = (
        P("expert", None),
        P("expert", None),
        P("expert", None),
        P("expert", None),
        P("expert", "dp", None),
        P("expert", "dp", None),
        P("expert", "dp", None),
    )
    return jax.shard_map(
        local,
        mesh=mesh,
        in_specs=placed,
        out_specs=(
            P("expert", "dp"),
            P("expert", "dp", None),
            P("expert", "dp", None),
            P("expert", "dp", None),
        ),
        check_vma=False,
    )
```

time: 453 us -> 136 us (0.30)
  the two profiles are of different devices: /device:TPU:2 before, /device:TPU:96 now
where the time goes in v1:
time: 136 us
  Pallas kernels  126 us (93%)
  local copies, waits for them, and re-layouts  7.51 us (6%)
  other arithmetic  1.94 us (1%)
    pallas_call x1, Pallas kernels, local(): pl.pallas_call(kernel, out_shape=(jax.ShapeDtypeStruct((TOK, BLOCK), BF16...  126 us
    unnamed x8, local copies, waits for them, and re-layouts  7.51 us

profile of v1, /device:TPU:96, one launch (start us, length us, event | category | flops | bytes accessed | tf_op | source)
XLA Modules:
  0.0 136.0 jit_solution(2194282096520101516)
XLA Ops:
  0.6 0.7 convert_element_type.3
  1.3 1.3 maximum_bitcast_fusion.route_ref
  2.6 125.9 %expert_backward.1 = (bf16[128,512]{1,0:T(8,128)(2,1)}, bf16[192,4096]{1,0:T(8,128)(2,1)}, bf16[192,4096]{1,0:T(8,128)(2,1)}, bf16[192,4096]{1,0:T(8,128)(2,1)}) custom-call(f32[4,128]{1,0:T(4,128)} %maximum_bitcast_fusion.route_ref, bf16[128,4096]{1,0:T(8,128)(2,1)} %tok_hbm.1, bf16[128,4096]{1,0:T(8,128)(2,1)} %cot_hbm.1, bf16[192,4096]{1,0:T(8,128)(2,1)} %bitcast.11, ...), custom_call_target="tpu_custom_call" | custom-call | tf_op jit(solution)/shard_map/expert_backward/pallas_call | solution.py:301
  128.5 1.6 %copy.15 = bf16[128,512]{1,0:T(8,128)(2,1)} copy(bf16[128,512]{1,0:T(8,128)(2,1)} %get-tuple-element.16) | data formatting | bytes 262144
  130.1 0.0 copy-start.1
  130.1 2.8 %copy.16 = bf16[1,192,4096]{2,1,0:T(8,128)(2,1)} copy(bf16[1,192,4096]{2,1,0:T(8,128)(2,1)} %bitcast.10) | data formatting | bytes 3145728
  132.9 0.0 copy-done.1
  132.9 0.0 copy-start
  132.9 1.1 copy.17
  134.0 0.8 copy-done
  134.9 1.1 copy.18
Async XLA Ops:
  130.1 2.8 %copy-start.1 = (bf16[192,4096]{1,0:T(8,128)(2,1)S(1)}, bf16[192,4096]{1,0:T(8,128)(2,1)}, u32[]{:S(2)}) copy-start(bf16[192,4096]{1,0:T(8,128)(2,1)} %get-tuple-element.10) | copy-start | bytes 4718596
  132.9 2.0 %copy-start = (bf16[192,4096]{1,0:T(8,128)(2,1)S(1)}, bf16[192,4096]{1,0:T(8,128)(2,1)}, u32[]{:S(2)}) copy-start(bf16[192,4096]{1,0:T(8,128)(2,1)} %get-tuple-element.11) | copy-start | bytes 4718596

commit v2 on v1

v2 whole, which is shorter than its diff:
```python
import functools

import jax
import jax.numpy as jnp
from jax import lax
from jax.experimental import pallas as pl
from jax.experimental.pallas import tpu as pltpu
from jax.sharding import PartitionSpec as P

MESH = pl.DeviceIdType.MESH
F32, BF16 = jnp.float32, jnp.bfloat16
D = 4096
HALF = 2048
QUARTER = 1024
BLOCK = 512
FF = 192
TOK = 128
CAP = 16
EXPERTS = 32
ROWS = EXPERTS * CAP
SIZES = (8, 8, 8, 8)
CHUNKS = len(SIZES)
FIRST = tuple(sum(SIZES[:ch]) for ch in range(CHUNKS))

Z_C = ((1, 0), (-1, 0), (2, 0), (0, 1), (-1, 1), (1, 1), (-2, 1), (0, 0))
ON_CHIP = ((0, 0, 1), (0, 0, 0))
MESSAGES = tuple(
    (dy,) + Z_C[(k + 2 * n) % 8]
    for k in range(8)
    for n, dy in enumerate((1, 3, 2, 0))
    if (dy,) + Z_C[(k + 2 * n) % 8] not in ON_CHIP
) + ON_CHIP
CORE, SELF = EXPERTS - 2, EXPERTS - 1
REMOTE = tuple(range(SELF))


def nt(left, right):
    return lax.dot_general(left, right, (((1,), (1,)), ((), ())), preferred_element_type=F32)


def nn(left, right):
    return lax.dot_general(left, right, (((1,), (0,)), ((), ())), preferred_element_type=F32)


def tn(left, right):
    return lax.dot_general(left, right, (((0,), (0,)), ((), ())), preferred_element_type=F32)


def ranks(routes):
    ids0, ids1 = routes[0:1, :], routes[1:2, :]
    expert_row = lax.broadcasted_iota(jnp.int32, (EXPERTS, TOK), 0).astype(F32)
    earlier = (
        lax.broadcasted_iota(jnp.int32, (TOK, TOK), 0)
        < lax.broadcasted_iota(jnp.int32, (TOK, TOK), 1)
    )
    earlier = jnp.where(earlier, 1.0, 0.0).astype(BF16)
    hot0 = jnp.where(expert_row == ids0, 1.0, 0.0)
    hot1 = jnp.where(expert_row == ids1, 1.0, 0.0)
    before0 = nn(hot0.astype(BF16), earlier)
    before1 = nn(hot1.astype(BF16), earlier) + jnp.sum(hot0, axis=1, keepdims=True)
    return (
        jnp.sum(hot0 * before0, axis=0, keepdims=True),
        jnp.sum(hot1 * before1, axis=0, keepdims=True),
    )


def kernel(
    ids_ref, gate_ref, tok_hbm, cot_hbm, wg_hbm, wu_hbm, wd_hbm,
    gt_ref, gg_hbm, gu_hbm, gd_hbm,
    tok, tok_q, weights, onehot, gates, sent, sent_q, arrived, slope, swish, act, ggrad, ugrad,
    part_own, part_out, part_in, summed, returned, combined, fin_out, fin_in, fin_out2, fin_in2, grads,
    tok_sem, tok_q_sem, w_sem, self_sem,
    a_send, a_recv, k_send, k_recv, x_send, x_recv, p_send, p_recv, r_send, r_recv, s_send, s_recv, g_sem,
):
    dp, ex = lax.axis_index("dp"), lax.axis_index("expert")
    h, x = dp // 4, dp % 4
    y, l, c = ex // 8, (ex // 2) % 4, ex % 2
    z = h * 4 + l
    p = x % 2
    q = 1 - p

    def at(dx, dy, dz, dc):
        zz = (z + dz + 8) % 8
        return (
            (zz // 4) * 4 + (x + dx + 4) % 4,
            ((y + dy + 4) % 4) * 8 + (zz % 4) * 2 + (c + dc) % 2,
        )

    def remote(src, dst, send, recv, *offset):
        return pltpu.make_async_remote_copy(
            src, dst, send, recv, device_id=at(*offset), device_id_type=MESH
        )

    ins, q_ins, w_ins = [], [], []
    for i, src in enumerate((tok_hbm, cot_hbm)):
        for j in range(4):
            to = pl.ds(j * BLOCK, BLOCK)
            cols = pl.ds(pl.multiple_of((2 * j + p) * BLOCK, BLOCK), BLOCK)
            ins.append(pltpu.make_async_copy(src.at[:, cols], tok.at[i, :, to], tok_sem.at[4 * i + j]))
            cols = pl.ds(pl.multiple_of((2 * j + q) * BLOCK, BLOCK), BLOCK)
            q_ins.append(pltpu.make_async_copy(src.at[:, cols], tok_q.at[i, :, to], tok_q_sem.at[4 * i + j]))
    for i, src in enumerate((wg_hbm, wu_hbm, wd_hbm)):
        for b in range(8):
            to = pl.ds((b // 2) * BLOCK, BLOCK)
            w_ins.append(
                pltpu.make_async_copy(
                    src.at[:, pl.ds(b * BLOCK, BLOCK)], weights.at[i, b % 2, :, to], w_sem.at[8 * i + b]
                )
            )
    for copy in ins + q_ins + w_ins:
        copy.start()

    barrier = pltpu.get_barrier_semaphore()
    peers = [(0,) + MESSAGES[i] for i in REMOTE]
    peers += [(0, dy, -dz, dc) for dy, dz, dc in MESSAGES if abs(dz) == 2]
    peers += [(1, 0, 0, 0), (-1, 0, 0, 0), (2, 0, 0, 0), (0, 0, 4, 0)]
    for peer in peers:
        pl.semaphore_signal(barrier, inc=1, device_id=at(*peer), device_id_type=MESH)

    route = jnp.concatenate([ids_ref[...].astype(F32), gate_ref[...]], axis=0)
    rank0, rank1 = ranks(route)
    slot_row = lax.broadcasted_iota(jnp.int32, (CAP, TOK), 0).astype(F32)

    def slots(ch):
        for i in range(FIRST[ch], FIRST[ch] + SIZES[ch]):
            dy, dz, dc = MESSAGES[i]
            expert = (((y + dy) % 4) * 8 + ((l + dz + 4) % 4) * 2 + (c + dc) % 2).astype(F32)
            is0 = (slot_row == rank0) & (route[0:1, :] == expert)
            is1 = (slot_row == rank1) & (route[1:2, :] == expert)
            rows = pl.ds(i * CAP, CAP)
            onehot[rows, :] = jnp.where(is0 | is1, 1.0, 0.0)
            gate = jnp.where(is0, route[2:3, :], 0.0) + jnp.where(is1, route[3:4, :], 0.0)
            gates[rows, :] = jnp.broadcast_to(jnp.sum(gate, axis=1, keepdims=True), (CAP, TOK))

    def chunk_rows(ch, less=0):
        return pl.ds(FIRST[ch] * CAP, SIZES[ch] * CAP - less)

    def out_copy(i, kind):
        rows = pl.ds(i * CAP, CAP)
        return remote(
            sent.at[kind, rows], arrived.at[p, kind, rows], a_send.at[kind, i], a_recv.at[kind, i], 0, *MESSAGES[i]
        )

    def core_copy(kind):
        return remote(
            sent_q.at[kind], arrived.at[q, kind, pl.ds(CORE * CAP, CAP)], k_send.at[kind], k_recv.at[kind], 0, 0, 0, 1
        )

    def send_slots(ch, kind):
        rows = chunk_rows(ch)
        picked = nn(onehot[rows, :].astype(BF16), tok[kind])
        if kind == 1:
            picked = picked * gates[rows, 0:1]
        picked = picked.astype(BF16)
        sent[kind, rows, :] = picked
        for i in range(FIRST[ch], FIRST[ch] + SIZES[ch]):
            if i == SELF:
                arrived[p, kind, pl.ds(SELF * CAP, CAP), :] = picked[(SELF - FIRST[ch]) * CAP :]
            else:
                out_copy(i, kind).start()

    def send_local(kind):
        rows = pl.ds(CORE * CAP, 2 * CAP)
        picked = nn(onehot[rows, :].astype(BF16), tok_q[kind])
        if kind == 1:
            picked = picked * gates[rows, 0:1]
        picked = picked.astype(BF16)
        sent_q[kind] = picked[0:CAP]
        core_copy(kind).start()
        arrived[q, kind, pl.ds(SELF * CAP, CAP), :] = picked[CAP:]

    def sides(rows, src, dst, send, recv):
        return [
            remote(src(rows, cols), dst(rows, cols), send(side), recv(side), dx, 0, 0, 0)
            for side, dx, cols in ((0, 1, pl.ds(0, QUARTER)), (1, -1, pl.ds(QUARTER, QUARTER)))
        ]

    def spread(ch, kind, half):
        ref = lambda rows, cols: arrived.at[half, kind, rows, cols]
        rows = chunk_rows(ch, 2 * CAP if ch == CHUNKS - 1 else 0)
        return sides(
            rows, ref, ref, lambda side: x_send.at[ch, kind, side], lambda side: x_recv.at[ch, kind, side]
        )

    def forward(ch, kind):
        for i in range(FIRST[ch], FIRST[ch] + SIZES[ch]):
            if i not in (CORE, SELF):
                out_copy(i, kind).wait_recv()
        for copy in spread(ch, kind, p):
            copy.start()

    def parts(ch):
        return sides(
            chunk_rows(ch), lambda rows, cols: part_out.at[rows, cols], lambda rows, cols: part_in.at[rows, cols],
            lambda side: p_send.at[ch, side], lambda side: p_recv.at[ch, side],
        )

    def wait_rows(ch, kind):
        for copy in spread(ch, kind, q):
            copy.wait_recv()
        if ch == CHUNKS - 1:
            out_copy(CORE, kind).wait_recv()
            core_copy(kind).wait_recv()

    def compute_tokens(ch):
        wait_rows(ch, 0)
        rows = chunk_rows(ch)
        gate_pre = nt(arrived[0, 0, rows, :], weights[0, 0]) + nt(arrived[1, 0, rows, :], weights[0, 1])
        up_pre = nt(arrived[0, 0, rows, :], weights[1, 0]) + nt(arrived[1, 0, rows, :], weights[1, 1])
        s = jax.nn.sigmoid(gate_pre)
        value = gate_pre * s
        act[rows, :] = (value * up_pre).astype(BF16)
        swish[rows, :] = value
        slope[rows, :] = up_pre * (s * (1.0 + gate_pre * (1.0 - s)))

    def compute_cotangents(ch):
        wait_rows(ch, 1)
        rows = chunk_rows(ch)
        act_grad = nt(arrived[0, 1, rows, :], weights[2, 0]) + nt(arrived[1, 1, rows, :], weights[2, 1])
        gate_grad = (act_grad * slope[rows, :]).astype(BF16)
        up_grad = (act_grad * swish[rows, :]).astype(BF16)
        ggrad[rows, :] = gate_grad
        ugrad[rows, :] = up_grad
        part_out[rows, :] = (nn(gate_grad, weights[0, q]) + nn(up_grad, weights[1, q])).astype(BF16)
        for copy in parts(ch):
            copy.start()
        part_own[rows, :] = nn(gate_grad, weights[0, p]) + nn(up_grad, weights[1, p])

    def back(i):
        dy, dz, dc = MESSAGES[i]
        rows = pl.ds(i * CAP, CAP)
        return remote(summed.at[rows], returned.at[rows], r_send.at[i], r_recv.at[i], 0, -dy, -dz, dc)

    own_rows = pl.ds(SELF * CAP, CAP)
    self_back = pltpu.make_async_copy(summed.at[own_rows], returned.at[own_rows], self_sem)

    def give_back(ch):
        for copy in parts(ch):
            copy.wait_recv()
        rows = chunk_rows(ch)
        summed[rows, :] = (part_own[rows, :] + part_in[rows, :].astype(F32)).astype(BF16)
        for i in range(FIRST[ch], FIRST[ch] + SIZES[ch]):
            if i == SELF:
                self_back.start()
            else:
                back(i).start()

    slots(0)
    for copy in ins:
        copy.wait()
    pl.semaphore_wait(barrier, len(peers))
    for ch in range(CHUNKS):
        if ch:
            slots(ch)
        send_slots(ch, 0)
        send_slots(ch, 1)
    for copy in q_ins:
        copy.wait()
    send_local(0)
    send_local(1)
    pick = onehot[...].T.astype(BF16)
    for ch in range(CHUNKS):
        forward(ch, 0)
        if ch == 0:
            for copy in w_ins:
                copy.wait()
        else:
            compute_cotangents(ch - 1)
        forward(ch, 1)
        compute_tokens(ch)
        if ch:
            give_back(ch - 1)
    compute_cotangents(CHUNKS - 1)
    give_back(CHUNKS - 1)

    outs = (gg_hbm, gu_hbm, gd_hbm)

    def grad_copy(i, b):
        return pltpu.make_async_copy(
            grads.at[i, b], outs[i].at[:, pl.ds(pl.multiple_of(b * BLOCK, BLOCK), BLOCK)], g_sem.at[i, b]
        )

    @pl.loop(0, 8)
    def _(b):
        half, cols = b % 2, pl.ds(pl.multiple_of((b // 2) * BLOCK, BLOCK), BLOCK)
        inputs = arrived[half, 0, :, cols]
        grads[0, b] = tn(ggrad[...], inputs).astype(BF16)
        grad_copy(0, b).start()
        grads[1, b] = tn(ugrad[...], inputs).astype(BF16)
        grad_copy(1, b).start()
        grads[2, b] = tn(act[...], arrived[half, 1, :, cols]).astype(BF16)
        grad_copy(2, b).start()

    self_back.wait()
    for i in REMOTE:
        back(i).wait_recv()

    j_x, j_z = x // 2, h

    def fin_x(k):
        return remote(fin_out.at[k], fin_in.at[k], s_send.at[k], s_recv.at[k], 2, 0, 0, 0)

    fin_z = remote(fin_out2, fin_in2, s_send.at[2], s_recv.at[2], 0, 0, 4, 0)

    def token_block(b_z, b_x):
        cols = pl.ds(pl.multiple_of((2 * b_z + b_x) * BLOCK, BLOCK), BLOCK)
        return nn(pick, returned[:, cols])

    for k, b_z in enumerate((1 - j_z, j_z)):
        fin_out[k] = token_block(b_z, 1 - j_x).astype(BF16)
        fin_x(k).start()
    for k, b_z in enumerate((1 - j_z, j_z)):
        combined[k] = token_block(b_z, j_x)
    fin_x(0).wait_recv()
    fin_out2[...] = (combined[0] + fin_in[0].astype(F32)).astype(BF16)
    fin_z.start()
    fin_x(1).wait_recv()
    total = combined[1] + fin_in[1].astype(F32)
    fin_z.wait_recv()
    gt_ref[...] = (total + fin_in2[...].astype(F32)).astype(BF16)

    for i in REMOTE:
        out_copy(i, 0).wait_send()
        out_copy(i, 1).wait_send()
        back(i).wait_send()
    for kind in range(2):
        core_copy(kind).wait_send()
    for ch in range(CHUNKS):
        for copy in spread(ch, 0, p) + spread(ch, 1, p) + parts(ch):
            copy.wait_send()
    for copy in (fin_x(0), fin_x(1), fin_z):
        copy.wait_send()

    @pl.loop(0, 8)
    def _(b):
        for i in range(3):
            grad_copy(i, b).wait()


PIECES = 2


def finish(*refs):
    ins, outs, held, in_sem, out_sem = refs[:3], refs[3:6], refs[6], refs[7], refs[8]
    copies = []
    for i in range(3):
        for k in range(PIECES):
            rows = pl.ds(k * (FF // PIECES), FF // PIECES)
            copies.append((
                pltpu.make_async_copy(ins[i].at[rows], held.at[i, rows], in_sem.at[i, k]),
                pltpu.make_async_copy(held.at[i, rows], outs[i].at[rows], out_sem.at[i, k]),
            ))
    for copy, _ in copies:
        copy.start()
    for copy, on in copies:
        copy.wait()
        on.start()
    for _, on in copies:
        on.wait()


def local(tokens_x, cotangent, expert_ids, gate_weights, w_gate, w_up, w_down):
    vmem = pl.BlockSpec(memory_space=pltpu.VMEM)
    anywhere = pl.BlockSpec(memory_space=pl.ANY)
    dma = pltpu.SemaphoreType.DMA
    grad = jax.ShapeDtypeStruct((FF, D), BF16)
    grad_tokens, *grads = pl.pallas_call(
        kernel,
        out_shape=(jax.ShapeDtypeStruct((TOK, BLOCK), BF16), grad, grad, grad),
        in_specs=[vmem] * 2 + [anywhere] * 5,
        out_specs=(vmem, anywhere, anywhere, anywhere),
        scratch_shapes=[
            pltpu.VMEM((2, TOK, HALF), BF16),
            pltpu.VMEM((2, TOK, HALF), BF16),
            pltpu.VMEM((3, 2, FF, HALF), BF16),
            pltpu.VMEM((ROWS, TOK), F32),
            pltpu.VMEM((ROWS, TOK), F32),
            pltpu.VMEM((2, ROWS, HALF), BF16),
            pltpu.VMEM((2, CAP, HALF), BF16),
            pltpu.VMEM((2, 2, ROWS, HALF), BF16),
            pltpu.VMEM((ROWS, FF), F32),
            pltpu.VMEM((ROWS, FF), F32),
            pltpu.VMEM((ROWS, FF), BF16),
            pltpu.VMEM((ROWS, FF), BF16),
            pltpu.VMEM((ROWS, FF), BF16),
            pltpu.VMEM((ROWS, HALF), F32),
            pltpu.VMEM((ROWS, HALF), BF16),
            pltpu.VMEM((ROWS, HALF), BF16),
            pltpu.VMEM((ROWS, HALF), BF16),
            pltpu.VMEM((ROWS, HALF), BF16),
            pltpu.VMEM((2, TOK, BLOCK), F32),
            pltpu.VMEM((2, TOK, BLOCK), BF16),
            pltpu.VMEM((2, TOK, BLOCK), BF16),
            pltpu.VMEM((TOK, BLOCK), BF16),
            pltpu.VMEM((TOK, BLOCK), BF16),
            pltpu.VMEM((3, 8, FF, BLOCK), BF16),
            dma((8,)), dma((8,)), dma((24,)), dma,
            dma((2, EXPERTS)), dma((2, EXPERTS)), dma((2,)), dma((2,)),
            dma((CHUNKS, 2, 2)), dma((CHUNKS, 2, 2)), dma((CHUNKS, 2)), dma((CHUNKS, 2)),
            dma((EXPERTS,)), dma((EXPERTS,)), dma((3,)), dma((3,)), dma((3, 8)),
        ],
        name="expert_backward",
        compiler_params=pltpu.CompilerParams(
            collective_id=0, has_side_effects=True, vmem_limit_bytes=56 * 2**20
        ),
    )(expert_ids.T, gate_weights.T, tokens_x, cotangent, w_gate[0], w_up[0], w_down[0])
    grad_gate, grad_up, grad_down = pl.pallas_call(
        finish,
        out_shape=(grad, grad, grad),
        in_specs=[anywhere] * 3,
        out_specs=[anywhere] * 3,
        scratch_shapes=[pltpu.VMEM((3, FF, D), BF16), dma((3, PIECES)), dma((3, PIECES))],
        name="finish",
        compiler_params=pltpu.CompilerParams(vmem_limit_bytes=56 * 2**20),
    )(*grads)
    return grad_tokens, grad_gate[None], grad_up[None], grad_down[None]


def solution(mesh):
    placed = (
        P("expert", None),
        P("expert", None),
        P("expert", None),
        P("expert", None),
        P("expert", "dp", None),
        P("expert", "dp", None),
        P("expert", "dp", None),
    )
    return jax.shard_map(
        local,
        mesh=mesh,
        in_specs=placed,
        out_specs=(
            P("expert", "dp"),
            P("expert", "dp", None),
            P("expert", "dp", None),
            P("expert", "dp", None),
        ),
        check_vma=False,
    )
```

time: 136 us -> 125 us (0.919)
  the two profiles are of different devices: /device:TPU:96 before, /device:TPU:2 now
where the time goes in v2:
time: 125 us
  Pallas kernels  124 us (99%)
    pallas_call x1, Pallas kernels, local(): pl.pallas_call(kernel, out_shape=(jax.ShapeDtypeStruct((TOK, BLOCK), BF16...  120 us
    pallas_call x1, Pallas kernels, local(): pl.pallas_call(finish, out_shape=(grad, grad, grad), in_specs=[anywhere]...  4 us

profile of v2, /device:TPU:2, one launch (start us, length us, event | category | flops | bytes accessed | tf_op | source)
XLA Modules:
  0.0 124.9 jit_solution(6072085046521581026)
XLA Ops:
  0.6 119.5 %expert_backward.1 = (bf16[128,512]{1,0:T(8,128)(2,1)}, bf16[192,4096]{1,0:T(8,128)(2,1)}, bf16[192,4096]{1,0:T(8,128)(2,1)}, bf16[192,4096]{1,0:T(8,128)(2,1)}) custom-call(s32[2,128]{1,0:T(2,128)} %bitcast.11, f32[2,128]{1,0:T(2,128)} %bitcast.12, bf16[128,4096]{1,0:T(8,128)(2,1)} %tok_hbm.1, bf16[128,4096]{1,0:T(8,128)(2,1)} %cot_hbm.1, ...), custom_call_target="tpu_custom_call" | custom-call | tf_op jit(solution)/shard_map/expert_backward/pallas_call | solution.py:367
  120.2 0.0 copy-start
  120.2 4.0 %finish.1 = (bf16[192,4096]{1,0:T(8,128)(2,1)}, bf16[192,4096]{1,0:T(8,128)(2,1)}, bf16[192,4096]{1,0:T(8,128)(2,1)}) custom-call(bf16[192,4096]{1,0:T(8,128)(2,1)} %get-tuple-element.12.refs_0_, bf16[192,4096]{1,0:T(8,128)(2,1)} %get-tuple-element.13.refs_1_, bf16[192,4096]{1,0:T(8,128)(2,1)} %get-tuple-element.14.refs_2_), custom_call_target="tpu_custom_call" | custom-call | tf_op jit(solution)/shard_map/finish/pallas_call | solution.py:407
  124.2 0.0 copy-done
  124.2 0.7 copy.12
Async XLA Ops:
  120.2 4.0 %copy-start = (bf16[128,512]{1,0:T(8,128)(2,1)S(1)}, bf16[128,512]{1,0:T(8,128)(2,1)}, u32[]{:S(2)}) copy-start(bf16[128,512]{1,0:T(8,128)(2,1)} %get-tuple-element.22) | copy-start | bytes 393220

commit v3 on v2

--- a/solution.py
+++ b/solution.py
@@ -18,7 +18,7 @@
 CAP = 16
 EXPERTS = 32
 ROWS = EXPERTS * CAP
-SIZES = (8, 8, 8, 8)
+SIZES = (4,4,4,4,4,4,4,4)
 CHUNKS = len(SIZES)
 FIRST = tuple(sum(SIZES[:ch]) for ch in range(CHUNKS))
 
@@ -27,7 +27,7 @@
 MESSAGES = tuple(
     (dy,) + Z_C[(k + 2 * n) % 8]
     for k in range(8)
-    for n, dy in enumerate((1, 3, 2, 0))
+    for n, dy in enumerate((1, 2, 3, 0))
     if (dy,) + Z_C[(k + 2 * n) % 8] not in ON_CHIP
 ) + ON_CHIP
 CORE, SELF = EXPERTS - 2, EXPERTS - 1
@@ -78,6 +78,7 @@
     z = h * 4 + l
     p = x % 2
     q = 1 - p
+    turn = 1 - 2 * c
 
     def at(dx, dy, dz, dc):
         zz = (z + dz + 8) % 8
@@ -124,7 +125,8 @@
     def slots(ch):
         for i in range(FIRST[ch], FIRST[ch] + SIZES[ch]):
             dy, dz, dc = MESSAGES[i]
-            expert = (((y + dy) % 4) * 8 + ((l + dz + 4) % 4) * 2 + (c + dc) % 2).astype(F32)
+            expert = ((y + turn * dy + 4) % 4) * 8 + ((l + turn * dz + 4) % 4) * 2 + (c + dc) % 2
+            expert = expert.astype(F32)
             is0 = (slot_row == rank0) & (route[0:1, :] == expert)
             is1 = (slot_row == rank1) & (route[1:2, :] == expert)
             rows = pl.ds(i * CAP, CAP)
@@ -136,9 +138,10 @@
         return pl.ds(FIRST[ch] * CAP, SIZES[ch] * CAP - less)
 
     def out_copy(i, kind):
+        dy, dz, dc = MESSAGES[i]
         rows = pl.ds(i * CAP, CAP)
         return remote(
-            sent.at[kind, rows], arrived.at[p, kind, rows], a_send.at[kind, i], a_recv.at[kind, i], 0, *MESSAGES[i]
+            sent.at[kind, rows], arrived.at[p, kind, rows], a_send.at[kind, i], a_recv.at[kind, i], 0, turn * dy, turn * dz, dc
         )
 
     def core_copy(kind):
@@ -228,8 +231,8 @@
 
     def back(i):
         dy, dz, dc = MESSAGES[i]
-        rows = pl.ds(i * CAP, CAP)
-        return remote(summed.at[rows], returned.at[rows], r_send.at[i], r_recv.at[i], 0, -dy, -dz, dc)
+        rows, sign = pl.ds(i * CAP, CAP), turn if dc else -turn
+        return remote(summed.at[rows], returned.at[rows], r_send.at[i], r_recv.at[i], 0, sign * dy, sign * dz, dc)
 
     own_rows = pl.ds(SELF * CAP, CAP)
     self_back = pltpu.make_async_copy(summed.at[own_rows], returned.at[own_rows], self_sem)
@@ -259,18 +262,19 @@
     send_local(0)
     send_local(1)
     pick = onehot[...].T.astype(BF16)
+    forward(0, 0)
+    forward(0, 1)
+    for copy in w_ins:
+        copy.wait()
     for ch in range(CHUNKS):
-        forward(ch, 0)
-        if ch == 0:
-            for copy in w_ins:
-                copy.wait()
-        else:
-            compute_cotangents(ch - 1)
-        forward(ch, 1)
+        if ch + 1 < CHUNKS:
+            forward(ch + 1, 0)
         compute_tokens(ch)
+        if ch + 1 < CHUNKS:
+            forward(ch + 1, 1)
+        compute_cotangents(ch)
         if ch:
             give_back(ch - 1)
-    compute_cotangents(CHUNKS - 1)
     give_back(CHUNKS - 1)
 
     outs = (gg_hbm, gu_hbm, gd_hbm)

time: 125 us -> 117 us (0.936); the launches traced: 125 us -> 115 us
  Pallas kernels: 124 us -> 113 us
    pallas_call x1, Pallas kernels: 120 us -> 109 us  [local(): pl.pallas_call(kernel, out_shape=(jax.ShapeDtypeStruct((TOK, BLOCK), BF16...]
where the time goes in v3:
time: 117 us; the launch traced here: 115 us
  Pallas kernels  113 us (97%)
    pallas_call x1, Pallas kernels, local(): pl.pallas_call(kernel, out_shape=(jax.ShapeDtypeStruct((TOK, BLOCK), BF16...  109 us
    pallas_call x1, Pallas kernels, local(): pl.pallas_call(finish, out_shape=(grad, grad, grad), in_specs=[anywhere]...  4 us

profile of v3, /device:TPU:2, one launch (start us, length us, event | category | flops | bytes accessed | tf_op | source)
XLA Modules:
  0.0 114.7 jit_solution(5087199139210039491)
XLA Ops:
  0.6 109.4 %expert_backward.1 = (bf16[128,512]{1,0:T(8,128)(2,1)}, bf16[192,4096]{1,0:T(8,128)(2,1)}, bf16[192,4096]{1,0:T(8,128)(2,1)}, bf16[192,4096]{1,0:T(8,128)(2,1)}) custom-call(s32[2,128]{1,0:T(2,128)} %bitcast.11, f32[2,128]{1,0:T(2,128)} %bitcast.12, bf16[128,4096]{1,0:T(8,128)(2,1)} %tok_hbm.1, bf16[128,4096]{1,0:T(8,128)(2,1)} %cot_hbm.1, ...), custom_call_target="tpu_custom_call" | custom-call | tf_op jit(solution)/shard_map/expert_backward/pallas_call | solution.py:371
  110.0 0.0 copy-start
  110.0 4.0 %finish.1 = (bf16[192,4096]{1,0:T(8,128)(2,1)}, bf16[192,4096]{1,0:T(8,128)(2,1)}, bf16[192,4096]{1,0:T(8,128)(2,1)}) custom-call(bf16[192,4096]{1,0:T(8,128)(2,1)} %get-tuple-element.12.refs_0_, bf16[192,4096]{1,0:T(8,128)(2,1)} %get-tuple-element.13.refs_1_, bf16[192,4096]{1,0:T(8,128)(2,1)} %get-tuple-element.14.refs_2_), custom_call_target="tpu_custom_call" | custom-call | tf_op jit(solution)/shard_map/finish/pallas_call | solution.py:411
  114.0 0.0 copy-done
  114.0 0.7 copy.12
Async XLA Ops:
  110.0 4.0 %copy-start = (bf16[128,512]{1,0:T(8,128)(2,1)S(1)}, bf16[128,512]{1,0:T(8,128)(2,1)}, u32[]{:S(2)}) copy-start(bf16[128,512]{1,0:T(8,128)(2,1)} %get-tuple-element.22) | copy-start | bytes 393220

commit v4 on v3

--- a/solution.py
+++ b/solution.py
@@ -18,7 +18,7 @@
 CAP = 16
 EXPERTS = 32
 ROWS = EXPERTS * CAP
-SIZES = (4,4,4,4,4,4,4,4)
+SIZES = (2, 2, 4, 4, 4, 4, 4, 4, 4)
 CHUNKS = len(SIZES)
 FIRST = tuple(sum(SIZES[:ch]) for ch in range(CHUNKS))
 

time: 117 us -> 119 us (1.017); the launches traced: 115 us -> 119 us
  Pallas kernels: 113 us -> 117 us
    pallas_call x1, Pallas kernels: 109 us -> 113 us  [local(): pl.pallas_call(kernel, out_shape=(jax.ShapeDtypeStruct((TOK, BLOCK), BF16...]
where the time goes in v4:
time: 119 us
  Pallas kernels  117 us (98%)
    pallas_call x1, Pallas kernels, local(): pl.pallas_call(kernel, out_shape=(jax.ShapeDtypeStruct((TOK, BLOCK), BF16...  113 us
    pallas_call x1, Pallas kernels, local(): pl.pallas_call(finish, out_shape=(grad, grad, grad), in_specs=[anywhere]...  4 us

profile of v4, /device:TPU:2, one launch (start us, length us, event | category | flops | bytes accessed | tf_op | source)
XLA Modules:
  0.0 118.7 jit_solution(6783100510985344486)
XLA Ops:
  0.6 113.3 %expert_backward.1 = (bf16[128,512]{1,0:T(8,128)(2,1)}, bf16[192,4096]{1,0:T(8,128)(2,1)}, bf16[192,4096]{1,0:T(8,128)(2,1)}, bf16[192,4096]{1,0:T(8,128)(2,1)}) custom-call(s32[2,128]{1,0:T(2,128)} %bitcast.11, f32[2,128]{1,0:T(2,128)} %bitcast.12, bf16[128,4096]{1,0:T(8,128)(2,1)} %tok_hbm.1, bf16[128,4096]{1,0:T(8,128)(2,1)} %cot_hbm.1, ...), custom_call_target="tpu_custom_call" | custom-call | tf_op jit(solution)/shard_map/expert_backward/pallas_call | solution.py:371
  114.0 0.0 copy-start
  114.0 4.0 %finish.1 = (bf16[192,4096]{1,0:T(8,128)(2,1)}, bf16[192,4096]{1,0:T(8,128)(2,1)}, bf16[192,4096]{1,0:T(8,128)(2,1)}) custom-call(bf16[192,4096]{1,0:T(8,128)(2,1)} %get-tuple-element.12.refs_0_, bf16[192,4096]{1,0:T(8,128)(2,1)} %get-tuple-element.13.refs_1_, bf16[192,4096]{1,0:T(8,128)(2,1)} %get-tuple-element.14.refs_2_), custom_call_target="tpu_custom_call" | custom-call | tf_op jit(solution)/shard_map/finish/pallas_call | solution.py:411
  118.0 0.0 copy-done
  118.0 0.7 copy.12
Async XLA Ops:
  114.0 4.0 %copy-start = (bf16[128,512]{1,0:T(8,128)(2,1)S(1)}, bf16[128,512]{1,0:T(8,128)(2,1)}, u32[]{:S(2)}) copy-start(bf16[128,512]{1,0:T(8,128)(2,1)} %get-tuple-element.22) | copy-start | bytes 393220
